TPU v7x, 32 devices: a whole 2x2x4 slice. The times are simulated.
32 devices in a mesh: view: 4 (over z), tx: 2 (over x), ty: 4 (over y, core).
Axes of the slice: x: 2, y: 2, z: 4, core: 2. Of those that a mesh axis runs over, the one named last changes fastest.
Arguments:
- estimate: float32 [32, 256, 128], P('tx', 'ty'), may hold values from 0.5 to 2
- recorded: float32 [8, 32, 256, 128], P('view', 'tx', 'ty'), may hold values from 0.25 to 8
- psf_x: float32 [8, 3, 31], P('view'), may hold values from 0.005 to 0.1
- psf_y: float32 [8, 3, 31], P('view'), may hold values from 0.005 to 0.1
- psf_z: float32 [8, 3, 61], P('view'), may hold values from 0.005 to 0.1
Outputs:
- deconvolved: float32 [32, 256, 128], P('tx', 'ty', 'view')
All inputs are finite; a program needn't handle non-finite values.
Results may differ from a plain program's by a relative error of at most 0.0001.
Values sent between devices are 32-bit elements; how exact they have to be, the bound alone decides.
A program may use at most 64 MiB of HBM per device.

v0:
```python
import functools

import jax
import jax.numpy as jnp
from jax import lax
from jax.experimental import pallas as pl
from jax.experimental.pallas import tpu as pltpu
from jax.sharding import PartitionSpec as P

ITERS = 2


def with_halo(cells, sides, width):
    for axis, dim in sides:
        count = lax.axis_size(axis)
        ends = count - 1
        head = lax.slice_in_dim(cells, 0, width, axis=dim)
        tail = lax.slice_in_dim(cells, cells.shape[dim] - width, cells.shape[dim], axis=dim)
        cells = jnp.concatenate(
            [
                lax.ppermute(tail, axis, [(i, (i + 1) % count) for i in range(ends)]),
                cells,
                lax.ppermute(head, axis, [((i + 1) % count, i) for i in range(ends)]),
            ],
            axis=dim,
        )
    return cells


def tables(kernels, rows_out, cols_in, offset_lead):
    taps = kernels.shape[2]
    offset = (
        lax.broadcasted_iota(jnp.int32, (rows_out, cols_in), 1)
        - lax.broadcasted_iota(jnp.int32, (rows_out, cols_in), 0)
        + offset_lead
    )
    picker = (offset[:, :, None] == lax.broadcasted_iota(jnp.int32, (1, 1, taps), 2)).astype(
        jnp.float32
    )
    return jnp.einsum("vrk,abk->vrab", kernels, picker, precision=lax.Precision.HIGHEST)


def finish(section_x, table_y, table_z):
    section_y = jnp.einsum("vryb,vrxbz->vrxyz", table_y, section_x, precision=lax.Precision.HIGHEST)
    return jnp.einsum("vrzc,vrxyc->vxyz", table_z, section_y, precision=lax.Precision.HIGHEST)


def shards(estimate, recorded, psf_x, psf_y, psf_z):
    halo_width = (psf_x.shape[2] - 1) // 2
    depth_reach = (psf_z.shape[2] - 1) // 2
    size_x, size_y, size_z = estimate.shape
    view_count = lax.axis_size("view")
    slab_len = size_z // view_count
    first_cell = lax.axis_index("view") * slab_len
    total_views = recorded.shape[0] * view_count
    back_x = tables(psf_x, size_x, size_x + 2 * halo_width, 0)
    back_y = tables(psf_y, size_y, size_y + 2 * halo_width, 0)
    back_z = tables(psf_z, size_z, size_z, depth_reach)
    fwd_x = tables(psf_x[:, :, ::-1], size_x, size_x + 2 * halo_width, 0)
    fwd_y = tables(psf_y[:, :, ::-1], size_y, size_y + 2 * halo_width, 0)
    fwd_z = tables(psf_z[:, :, ::-1], size_z, size_z, depth_reach)
    owned = lax.dynamic_slice_in_dim(estimate, first_cell, slab_len, 2)
    for iteration in range(ITERS):
        padded = with_halo(estimate, (("tx", 0), ("ty", 1)), halo_width)
        section_x = jnp.einsum("vrxa,abz->vrxbz", fwd_x, padded, precision=lax.Precision.HIGHEST)
        forward = finish(section_x, fwd_y, fwd_z)
        quotient = recorded / forward
        pad_ratio = with_halo(quotient, (("tx", 1), ("ty", 2)), halo_width)
        section_back = jnp.einsum(
            "vrxa,vabz->vrxbz", back_x, pad_ratio, precision=lax.Precision.HIGHEST
        )
        correction = finish(section_back, back_y, back_z)
        log_local = jnp.sum(jnp.log(correction), axis=0)
        log_total = lax.psum(log_local, "view")
        estimate = estimate * jnp.exp(log_total / total_views)
        owned = lax.dynamic_slice_in_dim(estimate, first_cell, slab_len, 2)
    return owned


def spread(kernels, out_cells, in_cells):
    taps = kernels.shape[1]
    offset = in_cells[None, :] - out_cells[:, None] + (taps - 1) // 2
    picker = (offset[:, :, None] == lax.broadcasted_iota(jnp.int32, (1, 1, taps), 2)).astype(
        jnp.float32
    )
    return jnp.einsum("rk,abk->rab", kernels, picker, precision=lax.Precision.HIGHEST)


MESH = pl.DeviceIdType.MESH


def place():
    me, x, t = lax.axis_index("view"), lax.axis_index("tx"), lax.axis_index("ty")
    y, c = t // 2, t % 2
    return me, x, y, c, 2 * y + (x + y) % 2, (c + y) % 2


def at_quarter(me, quarter, core):
    quarter = jnp.clip(quarter, 0, 3)
    y = quarter // 2
    return me, (quarter + y) % 2, 2 * y + core


def greet(barrier, device):
    pl.semaphore_signal(barrier, inc=1, device_id=device, device_id_type=MESH)


def remote(src, dst, send, recv, device):
    return pltpu.make_async_remote_copy(
        src_ref=src, dst_ref=dst, send_sem=send, recv_sem=recv, device_id=device, device_id_type=MESH
    )


def greet_sides(barrier, me, quarter, cores):
    @pl.when(quarter > 0)
    def _():
        for core in cores:
            greet(barrier, at_quarter(me, quarter - 1, core))

    @pl.when(quarter < 3)
    def _():
        for core in cores:
            greet(barrier, at_quarter(me, quarter + 1, core))

    return len(cores) * (jnp.minimum(quarter, 1) + jnp.minimum(3 - quarter, 1))


def clear_ends(out, quarter, pad, length):
    zeros = jnp.zeros((out.shape[0], pad, out.shape[2]), jnp.float32)

    @pl.when(quarter == 0)
    def _():
        out[:, :pad] = zeros

    @pl.when(quarter == 3)
    def _():
        out[:, pad + length :] = zeros


def halo_kernel(pad, field, out, sends, recvs, local):
    me, x, y, c, quarter, _ = place()
    length = field.shape[1]
    barrier = pltpu.get_barrier_semaphore()
    count = greet_sides(barrier, me, quarter, [c])
    inner = pltpu.make_async_copy(field, out.at[:, pl.ds(pad, length)], local)
    inner.start()
    pl.semaphore_wait(barrier, count)
    up = lambda: remote(
        field.at[:, pl.ds(length - pad, pad)], out.at[:, pl.ds(0, pad)],
        sends.at[0], recvs.at[0], at_quarter(me, quarter + 1, c),
    )
    down = lambda: remote(
        field.at[:, pl.ds(0, pad)], out.at[:, pl.ds(pad + length, pad)],
        sends.at[1], recvs.at[1], at_quarter(me, quarter - 1, c),
    )

    @pl.when(quarter < 3)
    def _():
        up().start()

    @pl.when(quarter > 0)
    def _():
        down().start()

    clear_ends(out, quarter, pad, length)
    inner.wait()

    @pl.when(quarter < 3)
    def _():
        up().wait_send()
        down().wait_recv()

    @pl.when(quarter > 0)
    def _():
        down().wait_send()
        up().wait_recv()


def fan_out(out, start, rows, pad, length, me, x, y, c, quarter, sends, recvs, base):
    half = out.shape[0] // 2
    here, there = pl.ds(start, rows), pl.ds(half + start, rows)
    everything = pl.ds(pad, length)
    sem = lambda k: (sends.at[base + k], recvs.at[base + k])
    sibling = lambda: remote(
        out.at[here, everything], out.at[there, everything], *sem(0), (me, x, 2 * y + 1 - c)
    )
    up = lambda: [
        remote(
            out.at[here, pl.ds(length, pad)], out.at[rows_to, pl.ds(0, pad)], *sem(k),
            at_quarter(me, quarter + 1, core),
        )
        for rows_to, core, k in ((here, c, 1), (there, 1 - c, 2))
    ]
    down = lambda: [
        remote(
            out.at[here, pl.ds(pad, pad)], out.at[rows_to, pl.ds(pad + length, pad)], *sem(k),
            at_quarter(me, quarter - 1, core),
        )
        for rows_to, core, k in ((here, c, 3), (there, 1 - c, 4))
    ]

    def begin():
        @pl.when(quarter < 3)
        def _():
            for copy in up():
                copy.start()

        @pl.when(quarter > 0)
        def _():
            for copy in down():
                copy.start()

        sibling().start()

    def end():
        sibling().wait()

        @pl.when(quarter < 3)
        def _():
            for copy in up():
                copy.wait_send()
            for copy in down():
                copy.wait_recv()

        @pl.when(quarter > 0)
        def _():
            for copy in down():
                copy.wait_send()
            for copy in up():
                copy.wait_recv()

    return begin, end


def enter_kernel(pad, tile, out, sends, recvs, local):
    me, x, y, c, quarter, goal = place()
    half, length, _ = tile.shape
    barrier = pltpu.get_barrier_semaphore()
    for dx, dc in ((0, 1), (1, 0), (1, 1)):
        greet(barrier, (me, (x + dx) % 2, 2 * y + (c + dc) % 2))
    across = (me, x, 2 * (1 - y))
    middle = (quarter == 1) | (quarter == 2)

    @pl.when(middle)
    def _():
        for core in range(2):
            greet(barrier, (across[0], across[1], across[2] + core))

    pl.semaphore_wait(barrier, 3 + 2 * jnp.minimum(quarter * (3 - quarter), 1))
    clear_ends(out, quarter, pad, length)
    target = out.at[pl.ds(0, half), pl.ds(pad, length)]
    stays = (goal == x) & (x == c)
    keep = lambda: pltpu.make_async_copy(tile, target, local)
    move = lambda: remote(tile, target, sends.at[0], recvs.at[0], (me, goal, 2 * y + x))

    @pl.when(stays)
    def _():
        keep().start()
        keep().wait()

    @pl.when(jnp.logical_not(stays))
    def _():
        move().start()
        move().wait()

    begin, end = fan_out(out, 0, half, pad, length, me, x, y, c, quarter, sends, recvs, 1)
    begin()
    end()


def reduce_slabs(logs, pair, held, came, sends, recvs, me, x, y, c, views):
    half = logs.shape[0] // 2
    slab = half // views
    base = views
    swaps = []
    for s in (2, 1, 3, 0):
        j = (me + s) % views
        swaps.append((s, j, remote(
            logs.at[pl.ds(half + slab * j, slab)], held.at[pl.ds(slab * j, slab)],
            sends.at[s], recvs.at[s], (me, x, 2 * y + 1 - c),
        )))
    for _, _, copy in swaps:
        copy.start()
    out = []
    for s, j, copy in swaps:
        copy.wait_recv()
        rows = pl.ds(slab * j, slab)
        pair[rows] = logs[rows] + held[rows]
        if s:
            push = remote(
                pair.at[rows], came.at[s - 1], sends.at[base + s - 1], recvs.at[base + s - 1],
                (j, x, 2 * y + c),
            )
            push.start()
            out.append((s, push))
    total = pair[pl.ds(slab * me, slab)]
    for s, push in out:
        push.wait_recv()
        total = total + came[s - 1]
    for _, _, copy in swaps:
        copy.wait_send()
    for _, push in out:
        push.wait_send()
    return total


def step_kernel(pad, views, scale, logs, old, out, pair, held, came, sends, recvs):
    me, x, y, c, quarter, _ = place()
    length = logs.shape[1]
    slab = old.shape[0] // views
    barrier = pltpu.get_barrier_semaphore()
    greet(barrier, (me, x, 2 * y + 1 - c))
    for s in range(1, views):
        greet(barrier, ((me + s) % views, x, 2 * y + c))
    count = greet_sides(barrier, me, quarter, [0, 1])
    pl.semaphore_wait(barrier, views + count)
    total = reduce_slabs(logs, pair, held, came, sends, recvs, me, x, y, c, views)
    base = 2 * views - 1
    rows = pl.ds(slab * me, slab)
    inner = pl.ds(pad, length)
    out[rows, inner] = old[rows] * jnp.exp(total * scale)
    spread = []
    for s in (2, 1, 3):
        spread.append((s, remote(
            out.at[rows, inner], out.at[rows, inner], sends.at[base + s - 1],
            recvs.at[base + s - 1], ((me + s) % views, x, 2 * y + c),
        )))
    for _, copy in spread:
        copy.start()
    base = base + views - 1
    pieces = [fan_out(out, slab * me, slab, pad, length, me, x, y, c, quarter, sends, recvs, base)]
    pieces[0][0]()
    clear_ends(out, quarter, pad, length)
    for s, copy in (spread[1], spread[2], spread[0]):
        source = (me - s) % views
        came_rows = pl.ds(slab * source, slab)
        remote(
            out.at[came_rows, inner], out.at[came_rows, inner], sends.at[2 * views - 1 + s - 1],
            recvs.at[2 * views - 1 + s - 1], (source, x, 2 * y + c),
        ).wait_recv()
        piece = fan_out(
            out, slab * source, slab, pad, length, me, x, y, c, quarter, sends, recvs, base + 5 * s
        )
        piece[0]()
        pieces.append(piece)
    for _, copy in spread:
        copy.wait_send()
    for _, end in pieces:
        end()


def leave_kernel(views, scale, logs, old, out, pair, held, came, packed, sends, recvs, local):
    me, x, y, c, quarter, _ = place()
    slab = logs.shape[0] // 2 // views
    width = logs.shape[2] // views
    barrier = pltpu.get_barrier_semaphore()
    for dv in range(views):
        for dx in range(2):
            for dc in range(2):
                if dv + dx + dc:
                    greet(barrier, ((me + dv) % views, (x + dx) % 2, 2 * y + (c + dc) % 2))
    pl.semaphore_wait(barrier, 4 * views - 1)
    total = reduce_slabs(logs, pair, held, came, sends, recvs, me, x, y, c, views)
    base = 2 * views - 1
    fresh = old[pl.ds(slab * me, slab)] * jnp.exp(total * scale)
    for j in range(views):
        packed[j] = jnp.concatenate(
            [fresh[i, :, width * j : width * (j + 1)] for i in range(slab)], axis=-1
        )
    goal = (x + y) % 2
    stays = (c == x) & (goal == c)
    copies = [
        remote(
            packed.at[(me + s) % views], out.at[me], sends.at[base + s], recvs.at[base + s],
            ((me + s) % views, c, 2 * y + goal),
        )
        for s in range(views)
    ]
    keep = pltpu.make_async_copy(packed.at[me], out.at[me], local)
    for copy in copies[1:]:
        copy.start()

    @pl.when(stays)
    def _():
        keep.start()
        keep.wait()

    @pl.when(jnp.logical_not(stays))
    def _():
        copies[0].start()
        copies[0].wait()

    for s in range(1, views):
        copies[s].wait_send()
        source = (me - s) % views
        remote(
            packed.at[source], out.at[source], sends.at[base + s], recvs.at[base + s],
            (source, c, 2 * y + goal),
        ).wait_recv()


def call(kernel, number, shape, scratch, sems, *arrays, local=False):
    space = pl.BlockSpec(memory_space=pltpu.VMEM)
    return pl.pallas_call(
        kernel,
        out_shape=jax.ShapeDtypeStruct(shape, jnp.float32),
        in_specs=[space] * len(arrays),
        out_specs=space,
        scratch_shapes=[pltpu.VMEM(size, jnp.float32) for size in scratch]
        + [pltpu.SemaphoreType.DMA((sems,))] * 2
        + ([pltpu.SemaphoreType.DMA] if local else []),
        compiler_params=pltpu.CompilerParams(
            collective_id=number, has_side_effects=True, vmem_limit_bytes=24 * 2**20
        ),
    )(*arrays)


def halves(value):
    high = value.astype(jnp.bfloat16)
    return high, (value - high.astype(jnp.float32)).astype(jnp.bfloat16)


def dot(a, b):
    return jnp.dot(a, b, preferred_element_type=jnp.float32)


def blur_kernel(quotient, *refs):
    field, table_y, table_z, table_x = refs[:4]
    seen = refs[4] if quotient else None
    out, along_y, along_z = refs[4 + quotient :]
    rank, size_x, length, depth = along_y.shape
    step = along_z.shape[0] // (rank * size_x)
    high, low = halves(table_y[...])
    rows_y = jnp.concatenate([high, high, low], axis=1)

    def stage_y(i, carry):
        high, low = halves(jnp.concatenate([field[2 * i], field[2 * i + 1]], axis=1))
        result = dot(rows_y, jnp.concatenate([high, low, high], axis=0))
        for r in range(rank):
            for k in range(2):
                along_y[r, 2 * i + k] = result[
                    length * r : length * (r + 1), depth * k : depth * (k + 1)
                ]
        return carry

    lax.fori_loop(0, size_x // 2, stage_y, 0, unroll=16)

    chunk = 8
    for r in range(rank):
        high, low = halves(table_z[r])
        columns_z = jnp.concatenate(
            [
                jnp.concatenate([high, high], axis=0),
                jnp.concatenate([low, jnp.zeros_like(low)], axis=0),
            ],
            axis=1,
        )

        def stage_z(i, carry):
            value = along_y[r, pl.ds(chunk * i, chunk)].reshape(chunk * length, depth)
            result = dot(jnp.concatenate(halves(value), axis=1), columns_z)
            result = result[:, :depth] + result[:, depth:]
            for k in range(chunk):
                start = pl.multiple_of((r * size_x + chunk * i + k) * step, 8)
                along_z[pl.ds(start, length)] = result[length * k : length * (k + 1)]
            return carry

        lax.fori_loop(0, size_x // chunk, stage_z, 0, unroll=4)

    high, low = halves(table_x[...])
    rows_x = jnp.concatenate([high, high, low], axis=1)

    def stage_x(i, carry):
        value = jnp.concatenate(
            [along_z[pl.ds(2 * i + k, rank * size_x, stride=step)] for k in range(2)], axis=1
        )
        high, low = halves(value)
        result = dot(rows_x, jnp.concatenate([high, low, high], axis=0))
        for k in range(2):
            part = result[:, depth * k : depth * (k + 1)]
            cells = pl.ds(2 * i + k, size_x, stride=length)
            out[cells] = seen[cells] / part if quotient else jnp.log(part)
        return carry

    lax.fori_loop(0, length // 2, stage_x, 0, unroll=16)


def local_blur(field, table_x, table_y, table_z, seen=None):
    rank, size_x, _ = table_x.shape
    length, depth = table_y.shape[1], field.shape[2]
    space = pl.BlockSpec(memory_space=pltpu.VMEM)
    arrays = [
        field,
        table_y.reshape(rank * length, -1),
        jnp.swapaxes(table_z, 1, 2),
        jnp.swapaxes(table_x, 0, 1).reshape(size_x, -1),
    ]
    if seen is not None:
        arrays.append(seen.reshape(size_x * length, depth))
    return pl.pallas_call(
        functools.partial(blur_kernel, seen is not None),
        out_shape=jax.ShapeDtypeStruct((size_x * length, depth), jnp.float32),
        in_specs=[space] * len(arrays),
        out_specs=space,
        scratch_shapes=[
            pltpu.VMEM((rank, size_x, length, depth), jnp.float32),
            pltpu.VMEM((rank * size_x * (length + 8), depth), jnp.float32),
        ],
        compiler_params=pltpu.CompilerParams(vmem_limit_bytes=32 * 2**20),
        cost_estimate=pl.CostEstimate(
            flops=6 * 10**9, bytes_accessed=8 * 2**20, transcendentals=size_x * length * depth
        ),
    )(*arrays).reshape(size_x, length, depth)


def quarters(estimate, recorded, psf_x, psf_y, psf_z):
    half, length, depth = estimate.shape
    size_x = 2 * half
    reach = (psf_x.shape[2] - 1) // 2
    pad = -(-reach // 8) * 8
    views = lax.axis_size("view")
    core = lax.axis_index("ty") % 2
    slab = half // views
    scale = 1.0 / (recorded.shape[0] * views)
    padded = (size_x, length + 2 * pad, depth)

    plane = ("tx", "ty")
    flat = lambda x, y, c: x * 4 + y * 2 + c
    every = [(x, y, c) for x in range(2) for y in range(2) for c in range(2)]
    chip = lambda y, c: (c + y) % 2
    own = [(flat(x, y, c), flat(chip(y, c), y, x)) for x, y, c in every]
    other = [(flat(x, y, c), flat(chip(y, c), y, 1 - x)) for x, y, c in every]

    row = lax.axis_index("tx")
    first_seen = lax.ppermute(
        lax.dynamic_index_in_dim(recorded, row, 0, keepdims=False), plane, own
    )
    second_seen = lax.ppermute(
        lax.dynamic_index_in_dim(recorded, 1 - row, 0, keepdims=False), plane, other
    )

    pick = lambda psf: lax.dynamic_index_in_dim(psf, core, 0, keepdims=False)
    psf_x, psf_y, psf_z = pick(psf_x), pick(psf_y), pick(psf_z)
    order_x = (lax.iota(jnp.int32, size_x) + half * core) % size_x
    out_y, in_y = lax.iota(jnp.int32, length), lax.iota(jnp.int32, length + 2 * pad) - pad
    all_z = lax.iota(jnp.int32, depth)
    fwd_x = spread(psf_x[:, ::-1], order_x, order_x)
    fwd_y = spread(psf_y[:, ::-1], out_y, in_y)
    fwd_z = spread(psf_z[:, ::-1], all_z, all_z)
    back_x = spread(psf_x, order_x, order_x)
    back_y = spread(psf_y, out_y, in_y)
    back_z = spread(psf_z, all_z, all_z)

    field = call(functools.partial(enter_kernel, pad), 1, padded, [], 6, estimate, local=True)
    seen = jnp.concatenate([first_seen, second_seen], axis=0)
    for iteration in range(ITERS):
        quotient = local_blur(field, fwd_x, fwd_y, fwd_z, seen)
        wide = call(
            functools.partial(halo_kernel, pad), 2 + 2 * iteration, padded, [], 2, quotient, local=True
        )
        logs = local_blur(wide, back_x, back_y, back_z)
        old = field[:half, pad : pad + length]
        scratch = [(half, length, depth)] * 2 + [(views - 1, slab, length, depth)]
        if iteration < ITERS - 1:
            field = call(
                functools.partial(step_kernel, pad, views, scale), 3 + 2 * iteration, padded,
                scratch, 8 * views - 2, logs, old,
            )
        else:
            packed = (views, length, depth)
            result = call(
                functools.partial(leave_kernel, views, scale), 3 + 2 * iteration, packed,
                scratch + [packed], 3 * views, logs, old, local=True,
            )
            result = result.reshape(views, length, slab, depth // views)
            return jnp.transpose(result, (0, 2, 1, 3)).reshape(half, length, depth // views)


def solution(mesh):
    sizes = mesh.shape
    split = (sizes["view"], sizes["tx"], sizes["ty"]) == (4, 2, 4)
    return jax.shard_map(
        quarters if split else shards,
        mesh=mesh,
        in_specs=(
            P("tx", "ty", None),
            P("view", "tx", "ty", None),
            P("view", None, None),
            P("view", None, None),
            P("view", None, None),
        ),
        out_specs=P("tx", "ty", "view"),
        check_vma=False,
    )
```

profile of v0, /device:TPU:0, one launch (start us, length us, event | category | flops | bytes accessed | tf_op | source)
XLA Modules:
  0.0 121.5 jit_solution(6603844721448145168)
XLA Ops:
  0.0 1.3 %dynamic-slice_bitcast_fusion.1 = (f32[16,64,128]{2,1,0:T(8,128)S(1)}, f32[16,64,128]{2,1,0:T(8,128)S(1)}) fusion(f32[2,16,64,128]{3,2,1,0:T(8,128)} %param.6, s32[]{:T(128)S(6)} %select_n.38, s32[]{:T(128)S(6)} %select_n.39), kind=kLoop, calls=%fused_computation.13 | loop fusion | bytes 2097160 | tf_op jit(solution)/shard_map/jit(dynamic_index_in_dim)/squeeze | solution.py:536
  1.3 0.7 collective-permute-start
  2.0 6.2 %collective-permute-start.1 = (f32[16,64,128]{2,1,0:T(8,128)S(1)}, f32[16,64,128]{2,1,0:T(8,128)S(1)}, u32[]{:S(2)}, u32[]{:S(2)}) collective-permute-start(f32[16,64,128]{2,1,0:T(8,128)S(1)} %get-tuple-element.6), channel_id=1, source_target_pairs={{0,1},{1,5},{2,7},{3,3},{4,0},{5,4},{6,6},{7,2},{8,9},{9,13},{10,1... | collective-permute-start | bytes 1572872 | tf_op jit(solution)/shard_map/ppermute | solution.py:538
  8.3 0.1 rev.10
  8.4 0.1 rev.11
  8.5 0.1 rev.9
  8.6 0.1 subtract_add_fusion.2
  8.7 1.2 convolution_bitcast_fusion
  9.9 1.2 convolution_bitcast_fusion.1
  11.1 0.1 reshape.132.refs_3_
  11.2 0.1 reshape.136.refs_3_
  11.3 0.4 fusion.4
  11.7 0.4 fusion.5
  12.2 0.0 copy-start.1
  12.2 1.4 %fusion.1 = f32[3,128,128]{2,0,1:T(4,128)S(1)} fusion(s32[128,128]{1,0:T(8,128)S(1)} %subtract_add_fusion, f32[3,61]{1,0:T(4,128)S(1)} %rev.10), kind=kOutput, calls=%fused_computation.2 | convolution fusion | flops 36978688 | bytes 262876 | tf_op jit(solution)/shard_map/rk,abk->rab/dot_general | solution.py:86
  13.6 0.1 copy.35
  13.8 1.4 %fusion = f32[3,128,128]{2,0,1:T(4,128)S(1)} fusion(s32[128,128]{1,0:T(8,128)S(1)} %subtract_add_fusion, f32[1,3,61]{2,0,1:T(1,128)S(1)} %constant_dynamic-slice_fusion.1), kind=kOutput, calls=%fused_computation.1 | convolution fusion | flops 36978688 | bytes 262876 | tf_op jit(solution)/shard_map/rk,abk->rab/dot_general | solution.py:86
  15.2 0.1 copy.37
  15.3 16.5 %shard_map.55.refs_0_ = f32[32,96,128]{2,1,0:T(8,128)S(1)} custom-call(f32[16,64,128]{2,1,0:T(8,128)S(1)} %copy-done.1), custom_call_target="tpu_custom_call" | custom-call | tf_op jit(solution)/shard_map/pallas_call | solution.py:404
  31.9 0.0 collective-permute-done
  31.9 0.0 collective-permute-done.1
  31.9 0.1 pad_maximum_fusion
  32.0 3.8 %shard_map.56 = f32[2048,128]{1,0:T(8,128)S(1)} custom-call(f32[32,96,128]{2,1,0:T(8,128)S(1)} %shard_map.55.refs_0_, f32[192,96]{1,0:T(8,128)S(1)} %bitcast.57, f32[3,128,128]{2,1,0:T(8,128)S(1)} %bitcast.53, f32[32,96]{1,0:T(8,128)S(1)} %reshape.132.refs_3_, f32[2048,128]{1,0:T(8,128)S(1)} %bitcast.46), custom_call_target="tpu_custom_call" | custom-call | flops 6000000000 | bytes 8388608 | tf_op jit(solution)/shard_map/pallas_call | solution.py:500
  35.8 9.0 %shard_map.57.refs_0_ = f32[32,96,128]{2,1,0:T(8,128)S(1)} custom-call(f32[32,64,128]{2,1,0:T(8,128)S(1)} %bitcast.49), custom_call_target="tpu_custom_call" | custom-call | tf_op jit(solution)/shard_map/pallas_call | solution.py:404
  44.9 3.4 %shard_map.58 = f32[2048,128]{1,0:T(8,128)S(1)} custom-call(f32[32,96,128]{2,1,0:T(8,128)S(1)} %shard_map.57.refs_0_, f32[192,96]{1,0:T(8,128)S(1)} %bitcast.55, f32[3,128,128]{2,1,0:T(8,128)S(1)} %bitcast.51, f32[32,96]{1,0:T(8,128)S(1)} %reshape.136.refs_3_), custom_call_target="tpu_custom_call" | custom-call | flops 6000000000 | bytes 8388608 | tf_op jit(solution)/shard_map/pallas_call | solution.py:500
  48.3 31.9 %shard_map.59.refs_0_ = f32[32,96,128]{2,1,0:T(8,128)S(1)} custom-call(f32[32,64,128]{2,1,0:T(8,128)S(1)} %bitcast.45, f32[16,64,128]{2,1,0:T(8,128)S(1)} %slice.18.old), custom_call_target="tpu_custom_call" | custom-call | tf_op jit(solution)/shard_map/pallas_call | solution.py:404
  80.3 3.8 %shard_map.60 = f32[2048,128]{1,0:T(8,128)S(1)} custom-call(f32[32,96,128]{2,1,0:T(8,128)S(1)} %shard_map.59.refs_0_, f32[192,96]{1,0:T(8,128)S(1)} %bitcast.58, f32[3,128,128]{2,1,0:T(8,128)S(1)} %bitcast.54, f32[32,96]{1,0:T(8,128)S(1)} %reshape.132.refs_3_, f32[2048,128]{1,0:T(8,128)S(1)} %bitcast.47), custom_call_target="tpu_custom_call" | custom-call | flops 6000000000 | bytes 8388608 | tf_op jit(solution)/shard_map/pallas_call | solution.py:500
  84.1 8.6 %shard_map.61.refs_0_ = f32[32,96,128]{2,1,0:T(8,128)S(1)} custom-call(f32[32,64,128]{2,1,0:T(8,128)S(1)} %bitcast.48), custom_call_target="tpu_custom_call" | custom-call | tf_op jit(solution)/shard_map/pallas_call | solution.py:404
  92.7 3.4 %shard_map.62 = f32[2048,128]{1,0:T(8,128)S(1)} custom-call(f32[32,96,128]{2,1,0:T(8,128)S(1)} %shard_map.61.refs_0_, f32[192,96]{1,0:T(8,128)S(1)} %bitcast.56, f32[3,128,128]{2,1,0:T(8,128)S(1)} %bitcast.52, f32[32,96]{1,0:T(8,128)S(1)} %reshape.136.refs_3_), custom_call_target="tpu_custom_call" | custom-call | flops 6000000000 | bytes 8388608 | tf_op jit(solution)/shard_map/pallas_call | solution.py:500
  96.1 24.3 %shard_map.63 = f32[4,64,128]{2,1,0:T(8,128)S(1)} custom-call(f32[32,64,128]{2,1,0:T(8,128)S(1)} %bitcast.50, f32[16,64,128]{2,1,0:T(8,128)S(1)} %slice.19.old), custom_call_target="tpu_custom_call" | custom-call | tf_op jit(solution)/shard_map/pallas_call | solution.py:404
  120.4 0.2 fusion.14
  120.6 0.9 copy.39
  (21 shorter events, 0.2 us)
Async XLA Ops:
  0.0 8.3 %copy-start = (f32[2,3,61]{2,0,1:T(2,128)S(1)}, f32[2,3,61]{2,0,1:T(2,128)}, u32[]{:S(2)}) copy-start(f32[2,3,61]{2,0,1:T(2,128)} %param.9) | copy-start | bytes 4396
  0.0 8.4 %copy-start.3 = (f32[2,3,31]{2,0,1:T(2,128)S(1)}, f32[2,3,31]{2,0,1:T(2,128)}, u32[]{:S(2)}) copy-start(f32[2,3,31]{2,0,1:T(2,128)} %param.8) | copy-start | bytes 2236
  0.0 8.4 %copy-start.2 = (f32[2,3,31]{2,0,1:T(2,128)S(1)}, f32[2,3,31]{2,0,1:T(2,128)}, u32[]{:S(2)}) copy-start(f32[2,3,31]{2,0,1:T(2,128)} %param.7) | copy-start | bytes 2236
  1.3 30.6 %collective-permute-start = (f32[16,64,128]{2,1,0:T(8,128)S(1)}, f32[16,64,128]{2,1,0:T(8,128)S(1)}, u32[]{:S(2)}, u32[]{:S(2)}) collective-permute-start(f32[16,64,128]{2,1,0:T(8,128)S(1)} %get-tuple-element.5), channel_id=1, source_target_pairs={{0,0},{1,4},{2,6},{3,2},{4,1},{5,5},{6,7},{7,3},{8,8},{9,12},{10,1... | collective-permute-start | bytes 1572872 | tf_op jit(solution)/shard_map/ppermute | solution.py:535
  2.0 29.9 %collective-permute-start.1 = (f32[16,64,128]{2,1,0:T(8,128)S(1)}, f32[16,64,128]{2,1,0:T(8,128)S(1)}, u32[]{:S(2)}, u32[]{:S(2)}) collective-permute-start(f32[16,64,128]{2,1,0:T(8,128)S(1)} %get-tuple-element.6), channel_id=1, source_target_pairs={{0,1},{1,5},{2,7},{3,3},{4,0},{5,4},{6,6},{7,2},{8,9},{9,13},{10,1... | collective-permute-start | bytes 1572872 | tf_op jit(solution)/shard_map/ppermute | solution.py:538
  12.2 3.1 %copy-start.1 = (f32[16,64,128]{2,1,0:T(8,128)S(1)}, f32[16,64,128]{2,1,0:T(8,128)}, u32[]{:S(2)}) copy-start(f32[16,64,128]{2,1,0:T(8,128)} %tile.1) | copy-start | bytes 1572868
where the time goes:
time: 122 us
  Pallas kernels  105 us (86%)
  starting transfers between devices  6.87 us (6%)
  matrix products  6.05 us (5%)
  local copies, waits for them, and re-layouts  3.25 us (3%)
    pallas_call x5, Pallas kernels, call(): pl.pallas_call(kernel, out_shape=jax.ShapeDtypeStruct(shape, jnp.float32)...  90.4 us
    pallas_call x4, Pallas kernels, local_blur(): pl.pallas_call(functools.partial(blur_kernel, seen is not None), out_shap...  14.4 us
    ppermute x1, starting transfers between devices, quarters(): lax.ppermute(lax.dynamic_index_in_dim(recorded, 1 - row, 0, keepdims=Fals...  6.18 us
    dot_general x6, matrix products, spread(): jnp.einsum('rk,abk->rab', kernels, picker, precision=lax.Precision.HIGHEST)  6.05 us
  transfers between devices with their start and end apart: 2, of which 0 were waited for; matrix products, arithmetic and copies ran while one was open for 6% of the time, Pallas kernels for 14%

commit v1 on v0

--- a/solution.py
+++ b/solution.py
@@ -544,12 +544,11 @@
     order_x = (lax.iota(jnp.int32, size_x) + half * core) % size_x
     out_y, in_y = lax.iota(jnp.int32, length), lax.iota(jnp.int32, length + 2 * pad) - pad
     all_z = lax.iota(jnp.int32, depth)
-    fwd_x = spread(psf_x[:, ::-1], order_x, order_x)
     fwd_y = spread(psf_y[:, ::-1], out_y, in_y)
-    fwd_z = spread(psf_z[:, ::-1], all_z, all_z)
     back_x = spread(psf_x, order_x, order_x)
     back_y = spread(psf_y, out_y, in_y)
     back_z = spread(psf_z, all_z, all_z)
+    fwd_x, fwd_z = jnp.swapaxes(back_x, 1, 2), jnp.swapaxes(back_z, 1, 2)
 
     field = call(functools.partial(enter_kernel, pad), 1, padded, [], 6, estimate, local=True)
     seen = jnp.concatenate([first_seen, second_seen], axis=0)

time: 122 us -> 122 us (level)
  Pallas kernels: 105 us -> 108 us
  matrix products: 6.05 us -> 3.46 us
    pallas_call x5, Pallas kernels: 90.4 us -> 93.2 us  [call(): pl.pallas_call(kernel, out_shape=jax.ShapeDtypeStruct(shape, jnp.float32)...]
    dot_general x6 -> x4, matrix products: 6.05 us -> 3.46 us  [spread(): jnp.einsum('rk,abk->rab', kernels, picker, precision=lax.Precision.HIGHEST)]
  transfers between devices with their start and end apart: 2 -> 2, of which waited for: 0 -> 0; matrix products, arithmetic and copies ran while one was open for 6% -> 3% of each run, Pallas kernels for 14% -> 16%
where the time goes in v1:
time: 122 us
  Pallas kernels  108 us (89%)
  starting transfers between devices  6.87 us (6%)
  matrix products  3.46 us (3%)
  local copies, waits for them, and re-layouts  3 us (2%)
    pallas_call x5, Pallas kernels, call(): pl.pallas_call(kernel, out_shape=jax.ShapeDtypeStruct(shape, jnp.float32)...  93.2 us
    pallas_call x4, Pallas kernels, local_blur(): pl.pallas_call(functools.partial(blur_kernel, seen is not None), out_shap...  14.4 us
    ppermute x1, starting transfers between devices, quarters(): lax.ppermute(lax.dynamic_index_in_dim(recorded, 1 - row, 0, keepdims=Fals...  6.18 us
    dot_general x4, matrix products, spread(): jnp.einsum('rk,abk->rab', kernels, picker, precision=lax.Precision.HIGHEST)  3.46 us
  transfers between devices with their start and end apart: 2, of which 0 were waited for; matrix products, arithmetic and copies ran while one was open for 3% of the time, Pallas kernels for 16%

profile of v1, /device:TPU:0, one launch (start us, length us, event | category | flops | bytes accessed | tf_op | source)
XLA Modules:
  0.0 121.5 jit_solution(13219456271774019269)
XLA Ops:
  0.0 0.0 copy-start
  0.0 1.3 %dynamic-slice_bitcast_fusion.1 = (f32[16,64,128]{2,1,0:T(8,128)S(1)}, f32[16,64,128]{2,1,0:T(8,128)S(1)}) fusion(f32[2,16,64,128]{3,2,1,0:T(8,128)} %param.6, s32[]{:T(128)S(6)} %select_n.38, s32[]{:T(128)S(6)} %select_n.39), kind=kLoop, calls=%fused_computation.9 | loop fusion | bytes 2097160 | tf_op jit(solution)/shard_map/jit(dynamic_index_in_dim)/squeeze | solution.py:536
  1.3 0.7 collective-permute-start
  2.0 6.2 %collective-permute-start.1 = (f32[16,64,128]{2,1,0:T(8,128)S(1)}, f32[16,64,128]{2,1,0:T(8,128)S(1)}, u32[]{:S(2)}, u32[]{:S(2)}) collective-permute-start(f32[16,64,128]{2,1,0:T(8,128)S(1)} %get-tuple-element.6), channel_id=1, source_target_pairs={{0,1},{1,5},{2,7},{3,3},{4,0},{5,4},{6,6},{7,2},{8,9},{9,13},{10,1... | collective-permute-start | bytes 1572872 | tf_op jit(solution)/shard_map/ppermute | solution.py:538
  8.3 0.1 subtract_add_fusion.2
  8.3 0.0 copy-done
  8.4 0.0 copy-done.3
  8.4 0.0 copy-done.2
  8.4 1.2 fusion.6
  9.6 1.4 %fusion = f32[3,128,128]{2,0,1:T(4,128)S(1)} fusion(s32[128,128]{1,0:T(8,128)S(1)} %subtract_add_fusion, f32[1,3,61]{2,0,1:T(1,128)S(1)} %constant_dynamic-slice_fusion.1), kind=kOutput, calls=%fused_computation.1 | convolution fusion | flops 36978688 | bytes 262876 | tf_op jit(solution)/shard_map/rk,abk->rab/dot_general | solution.py:86
  11.0 0.1 copy.46
  11.2 0.1 rev.3
  11.3 0.1 reshape.136.refs_3_
  11.4 0.1 copy.43
  11.5 0.1 reshape.132.refs_3_
  11.6 0.4 fusion.3
  12.0 0.4 fusion.2
  12.5 0.0 copy-done.1
  12.5 19.4 %shard_map.55.refs_0_ = f32[32,96,128]{2,1,0:T(8,128)S(1)} custom-call(f32[16,64,128]{2,1,0:T(8,128)S(1)} %copy-done.1), custom_call_target="tpu_custom_call" | custom-call | tf_op jit(solution)/shard_map/pallas_call | solution.py:404
  31.9 0.0 collective-permute-done
  31.9 0.0 collective-permute-done.1
  31.9 0.1 pad_maximum_fusion
  32.0 3.8 %shard_map.56 = f32[2048,128]{1,0:T(8,128)S(1)} custom-call(f32[32,96,128]{2,1,0:T(8,128)S(1)} %shard_map.55.refs_0_, f32[192,96]{1,0:T(8,128)S(1)} %bitcast.40, f32[3,128,128]{2,1,0:T(8,128)S(1)} %copy.44.refs_2_, f32[32,96]{1,0:T(8,128)S(1)} %reshape.132.refs_3_, f32[2048,128]{1,0:T(8,128)S(1)} %bitcast.31), custom_call_target="tpu_custom_call" | custom-call | flops 6000000000 | bytes 8388608 | tf_op jit(solution)/shard_map/pallas_call | solution.py:500
  35.8 9.0 %shard_map.57.refs_0_ = f32[32,96,128]{2,1,0:T(8,128)S(1)} custom-call(f32[32,64,128]{2,1,0:T(8,128)S(1)} %bitcast.34), custom_call_target="tpu_custom_call" | custom-call | tf_op jit(solution)/shard_map/pallas_call | solution.py:404
  44.9 3.4 %shard_map.58 = f32[2048,128]{1,0:T(8,128)S(1)} custom-call(f32[32,96,128]{2,1,0:T(8,128)S(1)} %shard_map.57.refs_0_, f32[192,96]{1,0:T(8,128)S(1)} %bitcast.38, f32[3,128,128]{2,1,0:T(8,128)S(1)} %bitcast.36, f32[32,96]{1,0:T(8,128)S(1)} %reshape.136.refs_3_), custom_call_target="tpu_custom_call" | custom-call | flops 6000000000 | bytes 8388608 | tf_op jit(solution)/shard_map/pallas_call | solution.py:500
  48.3 31.6 %shard_map.59.refs_0_ = f32[32,96,128]{2,1,0:T(8,128)S(1)} custom-call(f32[32,64,128]{2,1,0:T(8,128)S(1)} %bitcast.30, f32[16,64,128]{2,1,0:T(8,128)S(1)} %slice.18.old), custom_call_target="tpu_custom_call" | custom-call | tf_op jit(solution)/shard_map/pallas_call | solution.py:404
  79.9 3.8 %shard_map.60 = f32[2048,128]{1,0:T(8,128)S(1)} custom-call(f32[32,96,128]{2,1,0:T(8,128)S(1)} %shard_map.59.refs_0_, f32[192,96]{1,0:T(8,128)S(1)} %bitcast.41, f32[3,128,128]{2,1,0:T(8,128)S(1)} %copy.44.refs_2_, f32[32,96]{1,0:T(8,128)S(1)} %reshape.132.refs_3_, f32[2048,128]{1,0:T(8,128)S(1)} %bitcast.32), custom_call_target="tpu_custom_call" | custom-call | flops 6000000000 | bytes 8388608 | tf_op jit(solution)/shard_map/pallas_call | solution.py:500
  83.7 8.9 %shard_map.61.refs_0_ = f32[32,96,128]{2,1,0:T(8,128)S(1)} custom-call(f32[32,64,128]{2,1,0:T(8,128)S(1)} %bitcast.33), custom_call_target="tpu_custom_call" | custom-call | tf_op jit(solution)/shard_map/pallas_call | solution.py:404
  92.6 3.4 %shard_map.62 = f32[2048,128]{1,0:T(8,128)S(1)} custom-call(f32[32,96,128]{2,1,0:T(8,128)S(1)} %shard_map.61.refs_0_, f32[192,96]{1,0:T(8,128)S(1)} %bitcast.39, f32[3,128,128]{2,1,0:T(8,128)S(1)} %bitcast.37, f32[32,96]{1,0:T(8,128)S(1)} %reshape.136.refs_3_), custom_call_target="tpu_custom_call" | custom-call | flops 6000000000 | bytes 8388608 | tf_op jit(solution)/shard_map/pallas_call | solution.py:500
  96.1 24.3 %shard_map.63 = f32[4,64,128]{2,1,0:T(8,128)S(1)} custom-call(f32[32,64,128]{2,1,0:T(8,128)S(1)} %bitcast.35, f32[16,64,128]{2,1,0:T(8,128)S(1)} %slice.19.old), custom_call_target="tpu_custom_call" | custom-call | tf_op jit(solution)/shard_map/pallas_call | solution.py:404
  120.4 0.2 fusion.14
  120.6 0.9 copy.49
  (16 shorter events, 0.2 us)
Async XLA Ops:
  0.0 8.3 %copy-start = (f32[2,3,61]{2,0,1:T(2,128)S(1)}, f32[2,3,61]{2,0,1:T(2,128)}, u32[]{:S(2)}) copy-start(f32[2,3,61]{2,0,1:T(2,128)} %param.9) | copy-start | bytes 4396
  0.0 8.4 %copy-start.3 = (f32[2,3,31]{2,0,1:T(2,128)S(1)}, f32[2,3,31]{2,0,1:T(2,128)}, u32[]{:S(2)}) copy-start(f32[2,3,31]{2,0,1:T(2,128)} %param.8) | copy-start | bytes 2236
  0.0 8.4 %copy-start.2 = (f32[2,3,31]{2,0,1:T(2,128)S(1)}, f32[2,3,31]{2,0,1:T(2,128)}, u32[]{:S(2)}) copy-start(f32[2,3,31]{2,0,1:T(2,128)} %param.7) | copy-start | bytes 2236
  1.3 30.6 %collective-permute-start = (f32[16,64,128]{2,1,0:T(8,128)S(1)}, f32[16,64,128]{2,1,0:T(8,128)S(1)}, u32[]{:S(2)}, u32[]{:S(2)}) collective-permute-start(f32[16,64,128]{2,1,0:T(8,128)S(1)} %get-tuple-element.5), channel_id=1, source_target_pairs={{0,0},{1,4},{2,6},{3,2},{4,1},{5,5},{6,7},{7,3},{8,8},{9,12},{10,1... | collective-permute-start | bytes 1572872 | tf_op jit(solution)/shard_map/ppermute | solution.py:535
  2.0 29.9 %collective-permute-start.1 = (f32[16,64,128]{2,1,0:T(8,128)S(1)}, f32[16,64,128]{2,1,0:T(8,128)S(1)}, u32[]{:S(2)}, u32[]{:S(2)}) collective-permute-start(f32[16,64,128]{2,1,0:T(8,128)S(1)} %get-tuple-element.6), channel_id=1, source_target_pairs={{0,1},{1,5},{2,7},{3,3},{4,0},{5,4},{6,6},{7,2},{8,9},{9,13},{10,1... | collective-permute-start | bytes 1572872 | tf_op jit(solution)/shard_map/ppermute | solution.py:538
  9.6 2.9 %copy-start.1 = (f32[16,64,128]{2,1,0:T(8,128)S(1)}, f32[16,64,128]{2,1,0:T(8,128)}, u32[]{:S(2)}) copy-start(f32[16,64,128]{2,1,0:T(8,128)} %tile.1) | copy-start | bytes 1572868
